TPU v7x, 512 devices: a whole 4x8x8 slice. The times are simulated.
512 devices in a mesh: seq: 32 (over x, z_hi, core), tensor: 16 (over z_lo, y).
Axes of the slice: x: 4, y: 8, z: 8 (z_hi: 4, z_lo: 2; z = z_hi * 2 + z_lo), core: 2. Of those that a mesh axis runs over, the one named last changes fastest.
Arguments:
- activations: bfloat16 [1, 4096, 4608], P(None, 'seq', 'tensor'), may hold values from -6 to 6
- adapter_down_weight: bfloat16 [4608, 16], P('tensor'), may hold values from -0.09375 to 0.09375
- queries: bfloat16 [1, 4096, 32, 128], P(None, 'seq', 'tensor'), may hold values from -21 to 21
- keys: bfloat16 [1, 4096, 16, 128], P(None, 'seq', 'tensor'), may hold values from -4.5 to 4.5
- values: bfloat16 [1, 4096, 16, 128], P(None, 'seq', 'tensor'), may hold values from -6 to 6
- sequence_lengths: int32 [1], replicated, may hold values from 2048 to 4096
- probe: float32 [4, 16, 32, 128], P(None, None, 'tensor', 'seq'), may hold values from -6 to 6
- basis: float32 [96, 16, 32, 128], P(None, None, 'tensor', 'seq'), may hold values from -6 to 6
Outputs:
- next_block: float32 [1, 4, 16, 32, 128], P(None, None, None, 'tensor', 'seq')
- block_diag: float32 [1, 4, 4], replicated
- block_sub: float32 [1, 4, 4], replicated
All inputs are finite; a program needn't handle non-finite values.
Results may differ from a plain program's by a relative error of at most 0.005.
Values may be sent and summed in bfloat16 or wider, within the bound.
A program may use at most 64 MiB of HBM per device.

v0:
```python
import jax
import jax.numpy as jnp
from jax import lax
from jax.sharding import PartitionSpec as P

QUERY_HEADS = 32
KEY_VALUE_HEADS = 16
HEAD_WIDTH = 128
ADAPTER_RANK = 16
STEPS = 1


adapter_scale = 0.25
query_scale = 144.0 ** (-0.5)
soft_cap = 50.0


def inner_mean(left, right):
    return jnp.dot(left, right.T, precision=lax.Precision.HIGHEST) / (
        ADAPTER_RANK * QUERY_HEADS * HEAD_WIDTH
    )


def on_device(
    activations, adapter_down_weight, queries, keys, values, sequence_lengths, probe, basis
):
    highest_precision = lax.Precision.HIGHEST
    seq_count = lax.axis_size("seq")
    batch_rows, local_len, local_heads, head_size = queries.shape
    query_group_width = QUERY_HEADS // KEY_VALUE_HEADS
    local_kv = local_heads // query_group_width
    padded_length = local_len * seq_count
    seq_share = probe.shape[3]
    gradient_factor = adapter_scale / (batch_rows * padded_length)
    partial_rank = jnp.dot(
        activations.reshape(batch_rows * local_len, -1),
        adapter_down_weight,
        preferred_element_type=jnp.float32,
    )
    rank_projection = lax.psum(partial_rank, "tensor").reshape(batch_rows, local_len, -1)
    grouped = queries.reshape(batch_rows, local_len, local_kv, query_group_width, head_size)
    row_index = lax.axis_index("seq") * local_len + jnp.arange(local_len, dtype=jnp.int32)
    valid_rows = row_index[None, :] < sequence_lengths[:, None]
    row_valid = valid_rows[None, :, None, None, :, None]

    def allowed_mask(count):
        col_index = jnp.arange(count, dtype=jnp.int32)
        usable = (col_index[None, None, :] <= row_index[None, :, None]) & (
            col_index[None, None, :] < sequence_lengths[:, None, None]
        )
        return usable[:, None, None]

    def capped_of(piece_keys):
        raw_scores = query_scale * jnp.einsum(
            "bigqd,bjgd->bgqij", grouped, piece_keys, preferred_element_type=jnp.float32
        )
        capped_tanh = jnp.tanh(raw_scores / soft_cap)
        return (soft_cap * capped_tanh, 1.0 - capped_tanh * capped_tanh)

    shard_part = lax.all_gather(keys, "seq", axis=1, tiled=True)
    key_mask = allowed_mask(shard_part.shape[1])
    logits, cap_slope = capped_of(shard_part)
    run_sum = jnp.sum(jnp.where(key_mask, jnp.exp(logits), 0.0), axis=-1)
    log_norm = jnp.log(run_sum)

    def weights_of(piece_keys):
        key_mask = allowed_mask(piece_keys.shape[1])
        logits, cap_slope = capped_of(piece_keys)
        weights = jnp.where(key_mask, jnp.exp(logits - log_norm[..., None]), 0.0)
        return (weights, weights * cap_slope)

    saved_blocks = [basis.reshape(basis.shape[0], -1), probe.reshape(probe.shape[0], -1)]
    new_blocks, diag_list, sub_list = ([], [], [])
    probe_count = probe.shape[0]
    full_probe = lax.all_gather(probe, "seq", axis=3, tiled=True)
    probe_blocks = full_probe.reshape(
        probe_count, full_probe.shape[1], local_kv, query_group_width, head_size
    )
    query_tangent = (
        adapter_scale
        * jnp.einsum(
            "bir,krgqd->kbgqid",
            rank_projection,
            probe_blocks,
            precision=highest_precision,
            preferred_element_type=jnp.float32,
        )
    ).astype(jnp.bfloat16)
    piece_keys = lax.all_gather(keys, "seq", axis=1, tiled=True)
    piece_values = lax.all_gather(values, "seq", axis=1, tiled=True)
    weights, sloped = weights_of(piece_keys)
    tangent_scores = query_scale * jnp.einsum(
        "kbgqid,bjgd->kbgqij", query_tangent, piece_keys, preferred_element_type=jnp.float32
    )
    scaled = sloped[None] * tangent_scores
    attended = jnp.einsum(
        "bgqij,bjgd->bgqid",
        weights.astype(jnp.bfloat16),
        piece_values,
        preferred_element_type=jnp.float32,
    )
    lifted = jnp.einsum(
        "kbgqij,bjgd->kbgqid",
        scaled.astype(jnp.bfloat16),
        piece_values,
        preferred_element_type=jnp.float32,
    )
    weight_sum = jnp.sum(scaled, axis=-1)
    attended, lifted, weight_sum = (attended, lifted, weight_sum)
    output_tangent = jnp.where(row_valid, lifted - weight_sum[..., None] * attended[None], 0.0)
    cotangent = output_tangent.astype(jnp.bfloat16)
    correlation = jnp.sum(output_tangent * attended[None], axis=-1)
    piece_keys = lax.all_gather(keys, "seq", axis=1, tiled=True)
    piece_values = lax.all_gather(values, "seq", axis=1, tiled=True)
    weights, sloped = weights_of(piece_keys)
    aligned = jnp.einsum(
        "kbgqid,bjgd->kbgqij", cotangent, piece_values, preferred_element_type=jnp.float32
    )
    pushed = sloped[None] * (aligned - correlation[..., None])
    query_grad = query_scale * jnp.einsum(
        "kbgqij,bjgd->kbgqid",
        pushed.astype(jnp.bfloat16),
        piece_keys,
        preferred_element_type=jnp.float32,
    )
    partial_grad = gradient_factor * jnp.einsum(
        "bir,kbgqid->krgqd",
        rank_projection,
        query_grad,
        precision=highest_precision,
        preferred_element_type=jnp.float32,
    )
    partial_grad = partial_grad.reshape(probe_count, partial_grad.shape[1], local_heads, head_size)
    total_grad = lax.psum(partial_grad, "seq")
    own_grad = lax.dynamic_slice_in_dim(total_grad, lax.axis_index("seq") * seq_share, seq_share, 3)
    residue = own_grad.reshape(probe_count, -1)
    stacked = jnp.concatenate(saved_blocks, axis=0)
    block_value = lax.psum(inner_mean(saved_blocks[-1], residue), ("seq", "tensor"))
    coeff_one = lax.psum(inner_mean(stacked, residue), ("seq", "tensor"))
    residue = residue - jnp.dot(coeff_one.T, stacked, precision=highest_precision)
    coeff_two = lax.psum(inner_mean(stacked, residue), ("seq", "tensor"))
    residue = residue - jnp.dot(coeff_two.T, stacked, precision=highest_precision)
    gram = lax.psum(inner_mean(residue, residue), ("seq", "tensor"))
    factor = jnp.linalg.cholesky(gram)
    next_vector = jax.scipy.linalg.solve_triangular(factor, residue, lower=True)
    diag_list.append(block_value)
    sub_list.append(factor.T)
    new_blocks.append(next_vector)
    saved_blocks.append(next_vector)
    next_block = jnp.stack(new_blocks).reshape((STEPS,) + probe.shape)
    return (next_block, jnp.stack(diag_list), jnp.stack(sub_list))


def solution(mesh):
    in_specs = (
        P(None, "seq", "tensor"),
        P("tensor", None),
        P(None, "seq", "tensor", None),
        P(None, "seq", "tensor", None),
        P(None, "seq", "tensor", None),
        P(),
        P(None, None, "tensor", "seq"),
        P(None, None, "tensor", "seq"),
    )
    out_specs = (P(None, None, None, "tensor", "seq"), P(), P())
    return jax.shard_map(
        on_device, mesh=mesh, in_specs=in_specs, out_specs=out_specs, check_vma=False
    )
```

profile of v0, /device:TPU:1, one launch (start us, length us, event | category | flops | bytes accessed | tf_op | source)
XLA Modules:
  0.0 713.1 jit_solution(5029617965256538032)
XLA Ops:
  7.2 0.0 copy-start
  7.2 0.0 all-gather.3.cloned.1.call-start
  7.2 0.7 all-gather.3.cloned.1.call-update
  7.9 0.0 all-gather.5.cloned.1.call-start
  8.0 1.5 copy.55
  9.4 0.0 all-gather.5.cloned.1.call-update
  9.4 0.0 all-reduce.3.cloned.1.call-start
  10.2 2.1 fusion.21
  12.3 0.0 copy-done
  12.3 0.8 fusion.53
  13.2 0.7 copy.52
  13.9 0.8 copy.86
  14.7 30.3 %psum.42 = f32[128,16]{0,1:T(8,128)S(1)} all-reduce(f32[128,16]{0,1:T(8,128)S(1)} %fusion.53), channel_id=1, replica_groups=mesh['seq'=32,'tensor'=16] {'tensor'}, use_global_device_ids=true, to_apply=%region_1.2 | all-reduce | flops 2048 | bytes 16384 | tf_op jit(solution)/shard_map/psum | solution.py:40
  45.1 58.4 %all_gather.13 = f32[4,16,2,128]{1,0,2,3:T(4,128)S(1)} all-gather(f32[4,16,2,4]{1,0,2,3:T(4,128)S(1)} %copy.52), channel_id=1, replica_groups=mesh['seq'=32,'tensor'=16] {'seq'}, dimensions={3}, use_global_device_ids=true | all-gather | bytes 67584 | tf_op jit(solution)/shard_map/all_gather | solution.py:75
  103.5 0.7 fusion.36
  104.2 0.0 all-gather.3.cloned.1.call-done
  104.2 2.7 fusion.14
  106.9 0.0 copy-start.2
  106.9 4.7 broadcast_multiply_fusion
  111.5 0.0 copy-done.2
  111.5 5.6 copy.54
  117.2 5.6 copy.51
  122.8 0.0 copy-start.3
  122.8 11.5 %all-gather.5.cloned.1.call-done = bf16[1,4096,1,128]{1,3,2,0:T(8,128)(2,1)} async-done(((bf16[1,128,1,128]{1,3,2,0:T(8,128)(2,1)}), bf16[1,4096,1,128]{1,3,2,0:T(8,128)(2,1)}) %all-gather.5.cloned.1.call-update) | async-done | bytes 1048592 | tf_op jit(solution)/shard_map/all_gather | solution.py:114
  134.3 0.0 copy-start.1
  134.3 3.6 fusion.19
  138.0 0.0 copy-done.3
  138.0 0.1 copy-done.1
  138.1 0.0 copy-start.4
  138.1 7.1 fusion.3
  145.1 0.0 copy-done.4
  145.1 8.8 %multiply_reduce_fusion = (f32[4,2,128]{2,1,0:T(2,128)S(1)}, bf16[4,1,1,2,128,128]{4,5,3,0,2,1:T(8,128)(2,1)S(1)}) fusion(f32[2,128,128]{1,2,0:T(8,128)S(1)} %fusion.19, f32[4,2,128]{2,1,0:T(2,128)S(1)} %get-tuple-element.20, bf16[1,4096,1,128]{1,3,2,0:T(8,128)(2,1)S(1)} %copy-done.4, f32[4,2,128,4096]{3,2,1,0:T(8,128)} %get-tuple-element.21, ...), kind=kOutput, calls=%fused_computation.55 | convolution fusion | flops 1082915840 | bytes 22421632 | tf_op jit(solution)/shard_map/kbgqij,bjgd->kbgqid/dot_general | solution.py:102
  153.9 0.0 copy-start.6
  153.9 0.0 copy-start.5
  154.0 6.9 fusion.26
  160.9 1.0 fusion.37
  161.9 0.0 all-reduce.3.cloned.1.call-update
  161.9 0.0 copy-done.6
  161.9 0.1 pad_maximum_fusion
  162.0 251.8 %all-reduce.3.cloned.1.call-done = f32[4,16,2,128]{3,1,2,0:T(8,128)} async-done(((f32[4,16,2,128]{3,1,2,0:T(8,128)}), f32[4,16,2,128]{3,1,2,0:T(8,128)}) %all-reduce.3.cloned.1.call-update) | async-done | bytes 65552 | tf_op jit(solution)/shard_map/psum | solution.py:134
  413.8 0.9 constant_dynamic-slice_fusion
  414.8 0.1 copy.68
  414.9 0.1 reshape.218
  415.0 0.2 convolution_multiply_fusion.5
  415.2 97.7 %psum.44 = f32[100,4]{0,1:T(4,128)S(1)} all-reduce(f32[100,4]{0,1:T(4,128)S(1)} %convolution_multiply_fusion.5), channel_id=1, replica_groups=mesh['seq'=32,'tensor'=16] {'seq','tensor'}, use_global_device_ids=true, to_apply=%region_5.6 | all-reduce | flops 400 | bytes 3200 | tf_op jit(solution)/shard_map/psum | solution.py:139
  512.9 0.2 convolution_subtract_fusion.1
  513.0 0.2 convolution_multiply_fusion.4
  513.2 93.6 %psum.45 = f32[100,4]{0,1:T(4,128)S(1)} all-reduce(f32[100,4]{0,1:T(4,128)S(1)} %convolution_multiply_fusion.4), channel_id=1, replica_groups=mesh['seq'=32,'tensor'=16] {'seq','tensor'}, use_global_device_ids=true, to_apply=%region_6.7 | all-reduce | flops 400 | bytes 3200 | tf_op jit(solution)/shard_map/psum | solution.py:141
  606.8 0.2 convolution_subtract_fusion
  607.0 0.2 convolution_multiply_fusion.3
  607.2 0.2 triangular_solve.38
  607.3 0.0 copy-done.5
  607.3 0.2 fusion.39
  607.5 0.1 copy.67
  607.6 95.3 %all-reduce = (f32[4,4]{0,1:T(4,128)S(1)}, f32[1,4,4]{2,1,0:T(4,128)}) all-reduce(f32[4,4]{0,1:T(4,128)S(1)} %convolution_multiply_fusion.3, f32[1,4,4]{2,1,0:T(4,128)S(1)} %fusion.39), channel_id=1, replica_groups=mesh['seq'=32,'tensor'=16] {'seq','tensor'}, use_global_device_ids=true, to_apply=%region_7.8 | all-reduce | flops 32 | bytes 256 | tf_op jit(solution)/shard_map/psum | solution.py:143
  702.9 0.1 copy.65
  703.0 0.4 cholesky.16
  703.4 0.6 compare_reduce_fusion
  704.0 0.6 fusion.61
  704.7 0.3 custom-call.7
  705.0 0.2 convolution_bitcast_fusion
  705.3 0.6 copy.72
  705.9 0.7 copy.71
  (7 shorter events, 0.1 us)
Async XLA Ops:
  7.2 5.2 copy-start
  7.2 97.0 %all-gather.3.cloned.1.call-start = ((), (), s32[]{:S(2)}) async-start(), calls=%async_computation | async-start | bytes 1081344 | tf_op jit(solution)/shard_map/all_gather | solution.py:113
  7.9 126.4 %all-gather.5.cloned.1.call-start = ((), (), s32[]{:S(2)}) async-start(), calls=%async_computation.1 | async-start | bytes 1081344 | tf_op jit(solution)/shard_map/all_gather | solution.py:114
  9.4 404.4 %all-reduce.3.cloned.1.call-start = ((), (), s32[]{:S(2)}) async-start(), calls=%async_computation.2 | async-start | bytes 131072 | tf_op jit(solution)/shard_map/psum | solution.py:134
  106.9 4.7 copy-start.2
  122.8 15.2 %copy-start.3 = (bf16[1,4096,1,128]{3,1,2,0:T(8,128)(2,1)S(1)}, bf16[1,4096,1,128]{3,1,2,0:T(8,128)(2,1)}, u32[]{:S(2)}) copy-start(bf16[1,4096,1,128]{3,1,2,0:T(8,128)(2,1)} %all-gather.3.cloned.1.call-done) | copy-start | bytes 3145732
  134.3 3.7 copy-start.1
  138.1 7.1 copy-start.4
  153.9 8.0 %copy-start.6 = (f32[96,16,2,4]{0,3,2,1:T(4,128)S(1)}, f32[96,16,2,4]{0,3,2,1:T(4,128)}, u32[]{:S(2)}) copy-start(f32[96,16,2,4]{0,3,2,1:T(4,128)} %param.15) | copy-start | bytes 147460
  153.9 453.4 %copy-start.5 = (f32[4,16,2,4]{1,3,2,0:T(4,128)S(1)}, f32[4,16,2,4]{1,3,2,0:T(4,128)}, u32[]{:S(2)}) copy-start(f32[4,16,2,4]{1,3,2,0:T(4,128)} %param.14) | copy-start | bytes 6148
Sparse Core Ops, SparseCore 0:
  11.1 64.7 all-gather.2
  79.0 55.2 all-gather.4
  162.1 251.7 all-reduce.2
where the time goes:
time: 714 us; the launch traced here: 713 us
  blocking collectives  375 us (53%)
  waiting for transfers between devices  264 us (37%)
  matrix products  32.9 us (5%)
  local copies, waits for them, and re-layouts  17.3 us (2%)
  between operations  14.6 us (2%)
  other arithmetic  8.93 us (1%)
    psum x1, waiting for transfers between devices, on_device(): total_grad = lax.psum(partial_grad, 'seq')  252 us
    psum x1, blocking collectives, on_device(): coeff_one = lax.psum(inner_mean(stacked, residue), ('seq', 'tensor'))  97.7 us
    psum x1, blocking collectives, on_device(): gram = lax.psum(inner_mean(residue, residue), ('seq', 'tensor'))  95.3 us
    psum x1, blocking collectives, on_device(): coeff_two = lax.psum(inner_mean(stacked, residue), ('seq', 'tensor'))  93.6 us
    all_gather x1, blocking collectives, on_device(): full_probe = lax.all_gather(probe, 'seq', axis=3, tiled=True)  58.4 us
    psum x1, blocking collectives, on_device(): lax.psum(partial_rank, 'tensor').reshape(batch_rows, local_len, -1)  30.3 us
  transfers between devices with their start and end apart: 3, of which 2 were waited for; matrix products, arithmetic and copies ran while one was open for 4% of the time, Pallas kernels for 0%

commit v1 on v0

v1 whole, which is shorter than its diff:
```python
import functools

import jax
import jax.numpy as jnp
from jax import lax
from jax.experimental import pallas as pl
from jax.experimental.pallas import tpu as pltpu
from jax.sharding import PartitionSpec as P

MESH = pl.DeviceIdType.MESH
HIGHEST = lax.Precision.HIGHEST
F32 = jnp.float32
BF16 = jnp.bfloat16

adapter_scale = 0.25
query_scale = 144.0 ** (-0.5)
soft_cap = 50.0

SEQ = 32
ROWS = 128
WIDTH = 128
RANK = 16
PROBES = 4
NB = 96
KNOWN = NB + PROBES
CHIPS = SEQ // 2
CHUNK = 2 * ROWS
GROUPS = 4
GROUP = ROWS // GROUPS
LANES = 128


def nn(a, b, precision=None):
    return lax.dot_general(
        a, b, (((1,), (0,)), ((), ())), precision=precision, preferred_element_type=F32
    )


def nt(a, b, precision=None):
    return lax.dot_general(
        a, b, (((1,), (1,)), ((), ())), precision=precision, preferred_element_type=F32
    )


def tn(a, b, precision=None):
    return lax.dot_general(
        a, b, (((0,), (0,)), ((), ())), precision=precision, preferred_element_type=F32
    )


def iota(shape, dim):
    return lax.broadcasted_iota(jnp.int32, shape, dim)


def spread(compact):
    lane = iota((PROBES, LANES), 1)
    own = (lane // 32) == iota((PROBES, LANES), 0)
    masked = [
        jnp.where(own, jnp.broadcast_to(compact[d : d + 1], (PROBES, LANES)), 0.0)
        for d in range(4)
    ]
    repeated = []
    for piece in masked:
        piece = piece + pltpu.roll(piece, 32, 1)
        repeated.append(piece + pltpu.roll(piece, 64, 1))
    return jnp.concatenate(masked, axis=1), jnp.concatenate(repeated, axis=1)


def kernel(
    tensor,
    act_hbm,
    down_hbm,
    q_hbm,
    k_hbm,
    v_hbm,
    len_ref,
    probe_hbm,
    basis_hbm,
    next_ref,
    diag_ref,
    sub_ref,
    act,
    down,
    qraw,
    qwide,
    qbuf,
    probe,
    basis,
    kv,
    lhs,
    acc,
    slopes,
    cot,
    corr,
    inv,
    grad,
    vect,
    wbuf,
    srep,
    gmat,
    lr_out,
    lr_in,
    lr,
    vt_out,
    vt_in,
    w_out,
    w_in,
    c_out,
    c_in,
    d_out,
    d_in,
    g_out,
    g_in,
    h_out,
    h_in,
    e_out,
    e_in,
    local_sem,
    kv_send,
    z_recv,
    x_recv,
    sib_recv,
    pair_send,
    pair_recv,
    ex_send,
    ex_recv,
):
    s = lax.axis_index("seq")
    t = lax.axis_index("tensor")
    x, z, core = s // 8, (s // 2) % 4, s % 2
    chip = s // 2
    partner = SEQ - 1 - s
    head = s // (SEQ // 2)

    def seq_at(xx, zz, cc):
        return (lax.rem(xx + 4, 4) * 4 + lax.rem(zz + 4, 4)) * 2 + cc

    loads = [
        pltpu.make_async_copy(src, dst, local_sem.at[i])
        for i, (src, dst) in enumerate(
            (
                (act_hbm, act),
                (down_hbm, down),
                (q_hbm, qraw),
                (probe_hbm, probe),
                (basis_hbm, basis),
                (k_hbm, kv.at[s, 0]),
                (v_hbm, kv.at[s, 1]),
            )
        )
    ]
    for load in loads:
        load.start()

    barrier = pltpu.get_barrier_semaphore()

    def greet_seq(o, carry):
        pl.semaphore_signal(
            barrier, inc=1, device_id={"seq": lax.rem(s + o, SEQ)}, device_id_type=MESH
        )
        return carry

    def greet_tensor(o, carry):
        pl.semaphore_signal(
            barrier,
            inc=1,
            device_id={"tensor": lax.rem(t + o, tensor)},
            device_id_type=MESH,
        )
        return carry

    lax.fori_loop(1, SEQ, greet_seq, 0)
    lax.fori_loop(1, tensor, greet_tensor, 0)
    pl.semaphore_wait(barrier, SEQ - 1 + tensor - 1)

    def send_seq(src_of, into, n):
        def body(o, carry):
            to = lax.rem(s + o, SEQ)
            pltpu.make_async_remote_copy(
                src_ref=src_of(to),
                dst_ref=into.at[s],
                send_sem=ex_send.at[n],
                recv_sem=ex_recv.at[n],
                device_id={"seq": to},
                device_id_type=MESH,
            ).start()
            return carry

        lax.fori_loop(1, SEQ, body, 0)

    def send_tensor(src, into, n):
        def body(o, carry):
            pltpu.make_async_remote_copy(
                src_ref=src,
                dst_ref=into.at[t],
                send_sem=ex_send.at[n],
                recv_sem=ex_recv.at[n],
                device_id={"tensor": lax.rem(t + o, tensor)},
                device_id_type=MESH,
            ).start()
            return carry

        lax.fori_loop(1, tensor, body, 0)

    def arrived(into, n):
        span = into.at[pl.ds(0, into.shape[0] - 1)]
        pltpu.make_async_copy(span, span, ex_recv.at[n]).wait()

    def sent(into, n):
        span = into.at[pl.ds(0, into.shape[0] - 1)]
        pltpu.make_async_copy(span, span, ex_send.at[n]).wait()

    def total(into):
        out = into[0]
        for i in range(1, into.shape[0]):
            out = out + into[i]
        return out

    def push(src, to, sem):
        pltpu.make_async_remote_copy(
            src_ref=src,
            dst_ref=src,
            send_sem=kv_send,
            recv_sem=sem,
            device_id={"seq": to},
            device_id_type=MESH,
        ).start()

    def came(ref, sem):
        pltpu.make_async_copy(ref, ref, sem).wait()

    z_up, z_down = seq_at(x, z + 1, core), seq_at(x, z + 3, core)
    x_up, x_down = seq_at(x + 1, z, core), seq_at(x + 3, z, core)
    sibling = seq_at(x, z, 1 - core)

    def push_column(d):
        src = kv.at[seq_at(x, z + d, core)]
        push(src, x_up, x_recv.at[d, 0])
        push(src, x_down, x_recv.at[d, 1])
        push(src, sibling, sib_recv.at[0, d])

    def pass_x(d):
        below = seq_at(x + 3, z + d, core)
        came(kv.at[below], x_recv.at[d, 0])
        push(kv.at[below, 0], x_up, x_recv.at[d, 2])
        push(kv.at[below], sibling, sib_recv.at[3, d])
        above = seq_at(x + 1, z + d, core)
        came(kv.at[above], x_recv.at[d, 1])
        push(kv.at[above, 1], x_down, x_recv.at[d, 3])
        push(kv.at[above], sibling, sib_recv.at[1, d])

    def pass_far(d):
        far = seq_at(x + 2, z + d, core)
        came(kv.at[far, 0], x_recv.at[d, 2])
        came(kv.at[far, 1], x_recv.at[d, 3])
        push(kv.at[far], sibling, sib_recv.at[2, d])

    loads[5].wait()
    loads[6].wait()
    mine = kv.at[s]
    push(mine, z_up, z_recv.at[0])
    push(mine, z_down, z_recv.at[1])
    push_column(0)

    loads[0].wait()
    loads[1].wait()
    partial = nn(down[...], act[...])
    lr_out[...] = partial
    lr_in[t] = partial
    send_tensor(lr_out, lr_in, 0)

    loads[3].wait()
    compact = jnp.concatenate(
        [probe[k, h] for k in range(PROBES) for h in range(2)], axis=1
    )
    vt_out[...] = compact
    vt_in[s] = compact
    send_seq(lambda to: vt_out, vt_in, 1)

    loads[2].wait()
    qwide[...] = qraw[...].astype(F32)
    qbuf[0] = qwide[pl.ds(head, ROWS, stride=2), :].astype(BF16)
    qbuf[2] = qwide[pl.ds(1 - head, ROWS, stride=2), :].astype(BF16)
    q_copy = pltpu.make_async_remote_copy(
        src_ref=qbuf.at[2],
        dst_ref=qbuf.at[1],
        send_sem=pair_send.at[0],
        recv_sem=pair_recv.at[0],
        device_id={"seq": partner},
        device_id_type=MESH,
    )
    q_copy.start()

    loads[4].wait()
    inner = iota((LANES, 4 * LANES), 0)
    outer = iota((LANES, 4 * LANES), 1)
    place = (
        (inner // 8 == outer % 16)
        & ((inner // 4) % 2 == (outer // 16) % 2)
        & (inner % 4 == outer // LANES)
    )
    srep[...] = jnp.zeros((LANES, 4 * LANES), F32)
    srep[0:NB] = tn(basis[...], place.astype(F32), HIGHEST)
    srep[NB:KNOWN] = spread(compact)[1]
    kinds = srep[...]
    gram = nt(kinds[:, :], kinds[:, :], HIGHEST) * (0.25 / (RANK * 2 * tensor * WIDTH))
    for i in range(SEQ):
        g_out[i] = gram[4 * i : 4 * i + 4]
    g_in[s] = g_out[s]
    send_seq(lambda to: g_out.at[to], g_in, 2)

    below = seq_at(x, z + 3, core)
    came(kv.at[below], z_recv.at[0])
    push(kv.at[below, 0], z_up, z_recv.at[2])
    push_column(3)
    above = seq_at(x, z + 1, core)
    came(kv.at[above], z_recv.at[1])
    push(kv.at[above, 1], z_down, z_recv.at[3])
    push_column(1)
    pass_x(0)
    far = seq_at(x, z + 2, core)
    came(kv.at[far, 0], z_recv.at[2])
    came(kv.at[far, 1], z_recv.at[3])
    push_column(2)

    arrived(lr_in, 0)
    lr[0] = total(lr_in)
    lr_copy = pltpu.make_async_remote_copy(
        src_ref=lr.at[0],
        dst_ref=lr.at[1],
        send_sem=pair_send.at[1],
        recv_sem=pair_recv.at[1],
        device_id={"seq": partner},
        device_id_type=MESH,
    )
    lr_copy.start()

    arrived(vt_in, 1)
    vect[...] = jnp.concatenate([vt_in[i] for i in range(SEQ)], axis=0).T
    q_copy.wait_recv()
    lr_copy.wait_recv()
    for b in range(2):
        for g in range(GROUPS):
            rows = pl.ds(g * GROUP, GROUP)
            lhs[b, g, 0:GROUP] = qbuf[b, rows]
        low = lr[b]
        for k in range(PROBES):
            vk = vect[pl.ds(pl.multiple_of(k * 32 + head * 16, 16), RANK), :]
            tangent = (adapter_scale * tn(low, vk, HIGHEST)).astype(BF16)
            for g in range(GROUPS):
                lhs[b, g, (k + 1) * GROUP : (k + 2) * GROUP] = tangent[
                    g * GROUP : (g + 1) * GROUP
                ]

    acc[...] = jnp.zeros(acc.shape, F32)
    ones = jnp.ones((CHUNK, WIDTH), BF16)
    length = len_ref[0]

    def first_of(b):
        return jnp.where(b == 0, s, partner) * ROWS

    def last_chunk(b):
        return jnp.where(b == 0, s, partner) // 2

    def keys_of(c):
        return jnp.concatenate([kv[2 * c, 0], kv[2 * c + 1, 0]], axis=0)

    def values_of(c):
        return jnp.concatenate([kv[2 * c, 1], kv[2 * c + 1, 1]], axis=0)

    def first_pass(b, c):
        keys = keys_of(c)
        ext = jnp.concatenate([values_of(c), ones], axis=1)
        for g in range(GROUPS):
            scores = nt(lhs[b, g], keys)
            capped = jnp.tanh(scores[0:GROUP] * (query_scale / soft_cap))
            row = first_of(b) + g * GROUP + iota((GROUP, 1), 0)
            limit = jnp.minimum(row, length - 1) - c * CHUNK
            weights = jnp.where(
                iota((GROUP, CHUNK), 1) <= limit, jnp.exp(soft_cap * capped), 0.0
            )
            sloped = weights * (1.0 - capped * capped)
            slopes[b, c, g] = sloped
            high = weights.astype(BF16)
            parts = [high, (weights - high.astype(F32)).astype(BF16)]
            for k in range(PROBES):
                parts.append(
                    (sloped * scores[(k + 1) * GROUP : (k + 2) * GROUP]).astype(BF16)
                )
            acc[b, g] += nn(jnp.concatenate(parts, axis=0), ext)

    def order(i):
        return jnp.where(i == 0, 0, jnp.where(i == 1, 3, i - 1))

    def column_step(p, carry):
        d = order(p)

        @pl.when(p > 0)
        def _():
            pass_x(d)

        def chunk_step(q, carry):
            e = order(q)

            @pl.when(q == 3)
            def _():
                pass_far(d)

            other = seq_at(x + e, z + d, 1 - core)
            came(kv.at[other], sib_recv.at[e, d])
            c = other // 2

            def block_step(b, carry):
                @pl.when(c <= last_chunk(b))
                def _():
                    first_pass(b, c)

                return carry

            return lax.fori_loop(0, 2, block_step, carry)

        return lax.fori_loop(0, 4, chunk_step, carry)

    lax.fori_loop(0, 4, column_step, 0)

    arrived(g_in, 2)
    piece = total(g_in)
    h_out[...] = piece
    h_in[t] = piece
    send_tensor(h_out, h_in, 3)

    def turn(b, carry):
        for g in range(GROUPS):
            full = acc[b, g]
            plain = full[0:GROUP] + full[GROUP : 2 * GROUP]
            share = 1.0 / plain[:, WIDTH:]
            attended = plain[:, :WIDTH] * share
            share_scaled = share * query_scale
            row = first_of(b) + g * GROUP + iota((GROUP, 1), 0)
            valid = row < length
            for k in range(PROBES):
                part = full[(k + 2) * GROUP : (k + 3) * GROUP]
                tangent = (part[:, :WIDTH] - part[:, WIDTH:] * attended) * share_scaled
                tangent = jnp.where(valid, tangent, 0.0)
                cot[b, g, k * GROUP : (k + 1) * GROUP] = tangent.astype(BF16)
                corr[b, g, k * GROUP : (k + 1) * GROUP] = jnp.broadcast_to(
                    jnp.sum(tangent * attended, axis=1, keepdims=True), (GROUP, WIDTH)
                )
            inv[b, g] = share * (query_scale * adapter_scale / (SEQ * ROWS))
        return carry

    lax.fori_loop(0, 2, turn, 0)

    grad[...] = jnp.zeros(grad.shape, F32)

    def second_pass(b, c):
        keys = keys_of(c)
        values = values_of(c)
        for g in range(GROUPS):
            aligned = nt(cot[b, g], values)
            sloped = slopes[b, c, g]
            parts = []
            for k in range(PROBES):
                level = corr[b, g, k * GROUP : (k + 1) * GROUP]
                level = jnp.concatenate([level, level], axis=1)
                parts.append(
                    (sloped * (aligned[k * GROUP : (k + 1) * GROUP] - level)).astype(
                        BF16
                    )
                )
            grad[b, g] += nn(jnp.concatenate(parts, axis=0), keys)

    def second_block(b, carry):
        def step(c, carry):
            second_pass(b, c)
            return carry

        return lax.fori_loop(0, last_chunk(b) + 1, step, carry)

    lax.fori_loop(0, 2, second_block, 0)

    wbuf[...] = jnp.zeros((LANES, WIDTH), F32)
    both = jnp.concatenate([lr[0], lr[1]], axis=1)
    for k in range(PROBES):
        stack = jnp.concatenate(
            [
                grad[b, g, k * GROUP : (k + 1) * GROUP] * inv[b, g]
                for b in range(2)
                for g in range(GROUPS)
            ],
            axis=0,
        )
        wbuf[pl.ds(pl.multiple_of(k * 32 + head * 16, 16), RANK), :] = nn(
            both, stack, HIGHEST
        )
    turned = wbuf[...].T
    for i in range(SEQ):
        w_out[i] = turned[4 * i : 4 * i + 4]
    w_in[s] = w_out[s]
    send_seq(lambda to: w_out.at[to], w_in, 4)

    arrived(h_in, 3)
    piece = total(h_in)
    e_out[...] = piece
    e_in[s] = piece
    send_seq(lambda to: e_out, e_in, 5)

    arrived(w_in, 4)
    masked, repeated = spread(total(w_in))
    srep[KNOWN : KNOWN + PROBES] = repeated
    dots = nt(masked, srep[...], HIGHEST) * (1.0 / (RANK * 2 * tensor * WIDTH))
    c_out[...] = dots
    c_in[s] = dots
    send_seq(lambda to: c_out, c_in, 6)

    arrived(e_in, 5)
    gmat[...] = jnp.concatenate([e_in[i] for i in range(SEQ)], axis=0)
    gfull = gmat[...]
    eye = (iota((LANES, LANES), 0) == iota((LANES, LANES), 1)).astype(F32)
    square = nn(gfull, gfull, HIGHEST)
    cube = nn(square, gfull, HIGHEST)
    once = 2.0 * eye - gfull
    twice = 4.0 * (eye + square) - 6.0 * gfull - cube

    arrived(c_in, 6)
    piece = total(c_in)
    d_out[...] = piece
    d_in[t] = piece
    send_tensor(d_out, d_in, 7)
    arrived(d_in, 7)
    dots = total(d_in)

    lane = iota((PROBES, LANES), 1)
    known = jnp.where(lane < KNOWN, dots, 0.0)
    coeff = nn(known, once, HIGHEST)
    quad = nn(known, twice, HIGHEST)
    pick = (lane == iota((PROBES, LANES), 0) + NB).astype(F32)
    small = nt(jnp.concatenate([quad, pick], axis=0), known, HIGHEST)
    gram = dots[:, KNOWN : KNOWN + PROBES] - small[0:PROBES]
    diag_ref[0] = small[PROBES:]

    low = [[None] * PROBES for _ in range(PROBES)]
    for j in range(PROBES):
        pivot = gram[j : j + 1, j : j + 1]
        for m in range(j):
            pivot = pivot - low[j][m] * low[j][m]
        low[j][j] = jnp.sqrt(pivot)
        for i in range(j + 1, PROBES):
            entry = gram[i : i + 1, j : j + 1]
            for m in range(j):
                entry = entry - low[i][m] * low[j][m]
            low[i][j] = entry / low[j][j]
    row4, col4 = iota((PROBES, PROBES), 0), iota((PROBES, PROBES), 1)
    upper = jnp.zeros((PROBES, PROBES), F32)
    for i in range(PROBES):
        for j in range(i + 1):
            upper = jnp.where((row4 == j) & (col4 == i), low[i][j], upper)
    sub_ref[0] = upper

    mix = jnp.where(
        lane < KNOWN,
        -coeff,
        (lane == iota((PROBES, LANES), 0) + KNOWN).astype(F32),
    )
    residue = nn(mix, srep[...], HIGHEST)
    rows = []
    for i in range(PROBES):
        row = residue[i : i + 1]
        for m in range(i):
            row = row - low[i][m] * rows[m]
        rows.append(row / low[i][i])
    lane1 = iota((1, LANES), 1) // 32
    made = []
    for d in range(4):
        row = rows[0][:, d * LANES : (d + 1) * LANES]
        for k in range(1, PROBES):
            row = jnp.where(lane1 == k, rows[k][:, d * LANES : (d + 1) * LANES], row)
        made.append(row)
    made = jnp.concatenate(made, axis=0)
    for k in range(PROBES):
        for h in range(2):
            at = k * 32 + h * 16
            next_ref[k, h] = made[:, at : at + 16]

    shards = kv.at[pl.ds(0, SEQ - 1)]
    pltpu.make_async_copy(shards, shards, kv_send).wait()
    q_copy.wait_send()
    lr_copy.wait_send()
    for n, into in enumerate((lr_in, vt_in, g_in, h_in, w_in, e_in, c_in, d_in)):
        sent(into, n)


def on_device(
    activations, adapter_down_weight, queries, keys, values, sequence_lengths, probe, basis
):
    tensor = lax.axis_size("tensor")
    width = activations.shape[2]
    act = activations.reshape(ROWS, width).T
    down = adapter_down_weight.T
    q = queries.reshape(2 * ROWS, WIDTH)
    k = keys.reshape(ROWS, WIDTH)
    v = values.reshape(ROWS, WIDTH)
    probe_in = probe.transpose(0, 2, 3, 1)
    basis_in = basis.transpose(1, 2, 3, 0).reshape(LANES, NB)
    anywhere = pl.BlockSpec(memory_space=pl.ANY)
    in_vmem = pl.BlockSpec(memory_space=pltpu.VMEM)
    piece = (4, LANES)
    by_seq = pltpu.VMEM((SEQ,) + piece, F32)
    by_tensor = pltpu.VMEM((tensor,) + piece, F32)
    one = pltpu.VMEM(piece, F32)
    turned, diag, sub = pl.pallas_call(
        functools.partial(kernel, tensor),
        out_shape=(
            jax.ShapeDtypeStruct((PROBES, 2, 4, RANK), F32),
            jax.ShapeDtypeStruct((1, PROBES, PROBES), F32),
            jax.ShapeDtypeStruct((1, PROBES, PROBES), F32),
        ),
        in_specs=[anywhere] * 5
        + [pl.BlockSpec(memory_space=pltpu.SMEM)]
        + [anywhere] * 2,
        out_specs=(in_vmem,) * 3,
        scratch_shapes=[
            pltpu.VMEM((width, ROWS), BF16),
            pltpu.VMEM((RANK, width), BF16),
            pltpu.VMEM((2 * ROWS, WIDTH), BF16),
            pltpu.VMEM((2 * ROWS, WIDTH), F32),
            pltpu.VMEM((3, ROWS, WIDTH), BF16),
            pltpu.VMEM((PROBES, 2, 4, RANK), F32),
            pltpu.VMEM((LANES, NB), F32),
            pltpu.VMEM((SEQ, 2, ROWS, WIDTH), BF16),
            pltpu.VMEM((2, GROUPS, (PROBES + 1) * GROUP, WIDTH), BF16),
            pltpu.VMEM((2, GROUPS, (PROBES + 2) * GROUP, 2 * WIDTH), F32),
            pltpu.VMEM((2, CHIPS, GROUPS, GROUP, CHUNK), F32),
            pltpu.VMEM((2, GROUPS, PROBES * GROUP, WIDTH), BF16),
            pltpu.VMEM((2, GROUPS, PROBES * GROUP, WIDTH), F32),
            pltpu.VMEM((2, GROUPS, GROUP, WIDTH), F32),
            pltpu.VMEM((2, GROUPS, PROBES * GROUP, WIDTH), F32),
            pltpu.VMEM((LANES, WIDTH), F32),
            pltpu.VMEM((LANES, WIDTH), F32),
            pltpu.VMEM((LANES, 4 * LANES), F32),
            pltpu.VMEM((LANES, LANES), F32),
            pltpu.VMEM((RANK, ROWS), F32),
            pltpu.VMEM((tensor, RANK, ROWS), F32),
            pltpu.VMEM((2, RANK, ROWS), F32),
            one,
            by_seq,
            by_seq,
            by_seq,
            one,
            by_seq,
            one,
            by_tensor,
            by_seq,
            by_seq,
            one,
            by_tensor,
            one,
            by_seq,
            pltpu.SemaphoreType.DMA((7,)),
            pltpu.SemaphoreType.DMA,
            pltpu.SemaphoreType.DMA((4,)),
            pltpu.SemaphoreType.DMA((4, 4)),
            pltpu.SemaphoreType.DMA((4, 4)),
            pltpu.SemaphoreType.DMA((2,)),
            pltpu.SemaphoreType.DMA((2,)),
            pltpu.SemaphoreType.DMA((8,)),
            pltpu.SemaphoreType.DMA((8,)),
        ],
        compiler_params=pltpu.CompilerParams(
            collective_id=0, has_side_effects=True, vmem_limit_bytes=40 * 1024 * 1024
        ),
    )(act, down, q, k, v, sequence_lengths, probe_in, basis_in)
    return turned.transpose(0, 3, 1, 2)[None], diag, sub


def solution(mesh):
    in_specs = (
        P(None, "seq", "tensor"),
        P("tensor", None),
        P(None, "seq", "tensor", None),
        P(None, "seq", "tensor", None),
        P(None, "seq", "tensor", None),
        P(),
        P(None, None, "tensor", "seq"),
        P(None, None, "tensor", "seq"),
    )
    out_specs = (P(None, None, None, "tensor", "seq"), P(), P())
    return jax.shard_map(
        on_device, mesh=mesh, in_specs=in_specs, out_specs=out_specs, check_vma=False
    )
```

time: 714 us -> 89.1 us (0.12)
  blocking collectives: 375 us -> 0 us
  waiting for transfers between devices: 264 us -> 0 us
  Pallas kernels: 0 us -> 80.7 us
  matrix products: 32.9 us -> 0 us
  between operations: 14.6 us -> 1.32 us
  local copies, waits for them, and re-layouts: 17.3 us -> 6.6 us
  other arithmetic: 8.93 us -> 0 us
    psum x4 -> x0, blocking collectives: 317 us -> none  [the longest x1 97.7 us: on_device(): coeff_one = lax.psum(inner_mean(stacked, residue), ('seq', 'tensor'))]
    psum x1 -> x0, waiting for transfers between devices: 252 us -> none  [on_device(): total_grad = lax.psum(partial_grad, 'seq')]
    pallas_call x0 -> x1, Pallas kernels: none -> 80.7 us  [on_device(): pl.pallas_call(functools.partial(kernel, tensor), out_shape=(jax.ShapeDty...]
    all_gather x1 -> x0, blocking collectives: 58.4 us -> none  [on_device(): full_probe = lax.all_gather(probe, 'seq', axis=3, tiled=True)]
    dot_general x14 -> x0, matrix products: 32.6 us -> none  [the longest x1 8.81 us: on_device(): jnp.einsum('kbgqij,bjgd->kbgqid', scaled.astype(jnp.bfloat16), piece_valu...]
    all_gather x2 -> x0, waiting for transfers between devices: 11.5 us -> none  [the longest x1 11.5 us: on_device(): piece_values = lax.all_gather(values, 'seq', axis=1, tiled=True)]
    mul x2 -> x0, local copies, waits for them, and re-layouts: 11.3 us -> none  [the longest x1 5.64 us: on_device(): pushed = sloped[None] * (aligned - correlation[..., None])]
  transfers between devices with their start and end apart: 3 -> 0, of which waited for: 2 -> 0; matrix products, arithmetic and copies ran while one was open for 4% -> 0% of each run, Pallas kernels for 0% -> 0%
where the time goes in v1:
time: 89.1 us; the launch traced here: 88.6 us
  Pallas kernels  80.7 us (91%)
  local copies, waits for them, and re-layouts  6.6 us (7%)
  between operations  1.32 us (1%)
    pallas_call x1, Pallas kernels, on_device(): pl.pallas_call(functools.partial(kernel, tensor), out_shape=(jax.ShapeDty...  80.7 us
    unnamed x17, local copies, waits for them, and re-layouts  6.6 us

profile of v1, /device:TPU:1, one launch (start us, length us, event | category | flops | bytes accessed | tf_op | source)
XLA Modules:
  0.0 88.6 jit_solution(12924678532364000589)
XLA Ops:
  0.6 0.0 copy-start.6
  1.3 0.0 copy-done.6
  1.3 0.0 copy-start
  1.3 0.9 copy-done
  2.2 0.0 copy-start.1
  2.2 0.8 copy-done.1
  3.1 0.0 copy-start.2
  3.1 0.8 copy-done.2
  3.9 0.0 copy-start.3
  3.9 0.8 copy-done.3
  4.7 0.0 copy-start.4
  4.7 0.8 copy-done.4
  5.4 0.0 copy-start.5
  5.4 0.7 copy-done.5
  6.1 80.7 %shard_map.103 = (f32[4,2,4,16]{3,2,1,0:T(4,128)S(1)}, f32[1,4,4]{2,1,0:T(4,128)S(1)}, f32[1,4,4]{2,1,0:T(4,128)S(1)}) custom-call(bf16[288,128]{1,0:T(8,128)(2,1)S(1)} %bitcast.14, bf16[16,288]{1,0:T(8,128)(2,1)S(1)} %bitcast.21, bf16[256,128]{1,0:T(8,128)(2,1)S(1)} %bitcast.15, bf16[128,128]{1,0:T(8,128)(2,1)S(1)} %bitcast.17, ...), custom_call_target="tpu_custom_call" | custom-call | tf_op jit(solution)/shard_map/pallas_call | solution.py:611
  86.8 0.6 copy.15
  87.4 0.6 copy.16
  88.0 0.6 copy.17
Async XLA Ops:
  0.6 0.7 copy-start.6
  1.3 0.9 copy-start
  2.2 0.8 copy-start.1
  3.1 0.8 copy-start.2
  3.9 0.8 copy-start.3
  4.7 0.8 copy-start.4
  5.4 0.7 copy-start.5

commit v2 on v1

--- a/solution.py
+++ b/solution.py
@@ -23,9 +23,9 @@
 PROBES = 4
 NB = 96
 KNOWN = NB + PROBES
-CHIPS = SEQ // 2
-CHUNK = 2 * ROWS
-GROUPS = 4
+CHUNK = 4 * ROWS
+CHUNKS = SEQ // 4
+GROUPS = 2
 GROUP = ROWS // GROUPS
 LANES = 128
 
@@ -76,9 +76,7 @@
     len_ref,
     probe_hbm,
     basis_hbm,
-    next_ref,
-    diag_ref,
-    sub_ref,
+    out_ref,
     act,
     down,
     qraw,
@@ -128,7 +126,6 @@
     s = lax.axis_index("seq")
     t = lax.axis_index("tensor")
     x, z, core = s // 8, (s // 2) % 4, s % 2
-    chip = s // 2
     partner = SEQ - 1 - s
     head = s // (SEQ // 2)
 
@@ -171,7 +168,6 @@
 
     lax.fori_loop(1, SEQ, greet_seq, 0)
     lax.fori_loop(1, tensor, greet_tensor, 0)
-    pl.semaphore_wait(barrier, SEQ - 1 + tensor - 1)
 
     def send_seq(src_of, into, n):
         def body(o, carry):
@@ -255,19 +251,11 @@
         came(kv.at[far, 1], x_recv.at[d, 3])
         push(kv.at[far], sibling, sib_recv.at[2, d])
 
-    loads[5].wait()
-    loads[6].wait()
-    mine = kv.at[s]
-    push(mine, z_up, z_recv.at[0])
-    push(mine, z_down, z_recv.at[1])
-    push_column(0)
-
     loads[0].wait()
     loads[1].wait()
     partial = nn(down[...], act[...])
     lr_out[...] = partial
     lr_in[t] = partial
-    send_tensor(lr_out, lr_in, 0)
 
     loads[3].wait()
     compact = jnp.concatenate(
@@ -275,12 +263,38 @@
     )
     vt_out[...] = compact
     vt_in[s] = compact
-    send_seq(lambda to: vt_out, vt_in, 1)
 
     loads[2].wait()
     qwide[...] = qraw[...].astype(F32)
     qbuf[0] = qwide[pl.ds(head, ROWS, stride=2), :].astype(BF16)
     qbuf[2] = qwide[pl.ds(1 - head, ROWS, stride=2), :].astype(BF16)
+
+    loads[4].wait()
+    inner = iota((LANES, 4 * LANES), 0)
+    outer = iota((LANES, 4 * LANES), 1)
+    place = (
+        (inner // 8 == outer % 16)
+        & ((inner // 4) % 2 == (outer // 16) % 2)
+        & (inner % 4 == outer // LANES)
+    )
+    srep[...] = jnp.zeros((LANES, 4 * LANES), F32)
+    srep[0:NB] = tn(basis[...], place.astype(F32), HIGHEST)
+    srep[NB:KNOWN] = spread(compact)[1]
+    kinds = srep[...]
+    gram = nt(kinds, kinds, HIGHEST) * (0.25 / (RANK * 2 * tensor * WIDTH))
+    for i in range(SEQ):
+        g_out[i] = gram[4 * i : 4 * i + 4]
+    g_in[s] = g_out[s]
+    loads[5].wait()
+    loads[6].wait()
+
+    pl.semaphore_wait(barrier, SEQ - 1 + tensor - 1)
+    mine = kv.at[s]
+    push(mine, z_up, z_recv.at[0])
+    push(mine, z_down, z_recv.at[1])
+    push_column(0)
+    send_tensor(lr_out, lr_in, 0)
+    send_seq(lambda to: vt_out, vt_in, 1)
     q_copy = pltpu.make_async_remote_copy(
         src_ref=qbuf.at[2],
         dst_ref=qbuf.at[1],
@@ -290,24 +304,6 @@
         device_id_type=MESH,
     )
     q_copy.start()
-
-    loads[4].wait()
-    inner = iota((LANES, 4 * LANES), 0)
-    outer = iota((LANES, 4 * LANES), 1)
-    place = (
-        (inner // 8 == outer % 16)
-        & ((inner // 4) % 2 == (outer // 16) % 2)
-        & (inner % 4 == outer // LANES)
-    )
-    srep[...] = jnp.zeros((LANES, 4 * LANES), F32)
-    srep[0:NB] = tn(basis[...], place.astype(F32), HIGHEST)
-    srep[NB:KNOWN] = spread(compact)[1]
-    kinds = srep[...]
-    gram = nt(kinds[:, :], kinds[:, :], HIGHEST) * (0.25 / (RANK * 2 * tensor * WIDTH))
-    for i in range(SEQ):
-        g_out[i] = gram[4 * i : 4 * i + 4]
-    g_in[s] = g_out[s]
-    send_seq(lambda to: g_out.at[to], g_in, 2)
 
     below = seq_at(x, z + 3, core)
     came(kv.at[below], z_recv.at[0])
@@ -318,10 +314,6 @@
     push(kv.at[above, 1], z_down, z_recv.at[3])
     push_column(1)
     pass_x(0)
-    far = seq_at(x, z + 2, core)
-    came(kv.at[far, 0], z_recv.at[2])
-    came(kv.at[far, 1], z_recv.at[3])
-    push_column(2)
 
     arrived(lr_in, 0)
     lr[0] = total(lr_in)
@@ -335,15 +327,22 @@
     )
     lr_copy.start()
 
+    far = seq_at(x, z + 2, core)
+    came(kv.at[far, 0], z_recv.at[2])
+    came(kv.at[far, 1], z_recv.at[3])
+    push_column(2)
+    pass_far(0)
+    pass_x(3)
+    pass_x(1)
+
     arrived(vt_in, 1)
     vect[...] = jnp.concatenate([vt_in[i] for i in range(SEQ)], axis=0).T
-    q_copy.wait_recv()
-    lr_copy.wait_recv()
-    for b in range(2):
+
+    def left_side(b):
+        low = lr[b]
+        query = qbuf[b]
         for g in range(GROUPS):
-            rows = pl.ds(g * GROUP, GROUP)
-            lhs[b, g, 0:GROUP] = qbuf[b, rows]
-        low = lr[b]
+            lhs[b, g, 0:GROUP] = query[g * GROUP : (g + 1) * GROUP]
         for k in range(PROBES):
             vk = vect[pl.ds(pl.multiple_of(k * 32 + head * 16, 16), RANK), :]
             tangent = (adapter_scale * tn(low, vk, HIGHEST)).astype(BF16)
@@ -352,6 +351,12 @@
                     g * GROUP : (g + 1) * GROUP
                 ]
 
+    left_side(0)
+    send_seq(lambda to: g_out.at[to], g_in, 2)
+    q_copy.wait_recv()
+    lr_copy.wait_recv()
+    left_side(1)
+
     acc[...] = jnp.zeros(acc.shape, F32)
     ones = jnp.ones((CHUNK, WIDTH), BF16)
     length = len_ref[0]
@@ -360,13 +365,13 @@
         return jnp.where(b == 0, s, partner) * ROWS
 
     def last_chunk(b):
-        return jnp.where(b == 0, s, partner) // 2
+        return jnp.where(b == 0, s, partner) // 4
 
     def keys_of(c):
-        return jnp.concatenate([kv[2 * c, 0], kv[2 * c + 1, 0]], axis=0)
+        return jnp.concatenate([kv[4 * c + i, 0] for i in range(4)], axis=0)
 
     def values_of(c):
-        return jnp.concatenate([kv[2 * c, 1], kv[2 * c + 1, 1]], axis=0)
+        return jnp.concatenate([kv[4 * c + i, 1] for i in range(4)], axis=0)
 
     def first_pass(b, c):
         keys = keys_of(c)
@@ -380,7 +385,7 @@
                 iota((GROUP, CHUNK), 1) <= limit, jnp.exp(soft_cap * capped), 0.0
             )
             sloped = weights * (1.0 - capped * capped)
-            slopes[b, c, g] = sloped
+            slopes[b, c, g * GROUP : (g + 1) * GROUP] = sloped
             high = weights.astype(BF16)
             parts = [high, (weights - high.astype(F32)).astype(BF16)]
             for k in range(PROBES):
@@ -389,26 +394,25 @@
                 )
             acc[b, g] += nn(jnp.concatenate(parts, axis=0), ext)
 
-    def order(i):
-        return jnp.where(i == 0, 0, jnp.where(i == 1, 3, i - 1))
-
-    def column_step(p, carry):
-        d = order(p)
-
-        @pl.when(p > 0)
+    def column_step(q, carry):
+        e = jnp.where(q == 0, 0, jnp.where(q == 1, 3, q - 1))
+
+        @pl.when(q == 1)
         def _():
-            pass_x(d)
-
-        def chunk_step(q, carry):
-            e = order(q)
-
-            @pl.when(q == 3)
-            def _():
-                pass_far(d)
-
-            other = seq_at(x + e, z + d, 1 - core)
-            came(kv.at[other], sib_recv.at[e, d])
-            c = other // 2
+            pass_x(2)
+            pass_far(3)
+            pass_far(1)
+
+        @pl.when(q == 3)
+        def _():
+            pass_far(2)
+
+        def pair_step(p, carry):
+            pair = lax.rem(z // 2 + p, 2)
+            for i in range(2):
+                other = seq_at(x + e, 2 * pair + i, 1 - core)
+                came(kv.at[other], sib_recv.at[e, lax.rem(2 * pair + i - z + 4, 4)])
+            c = seq_at(x + e, 2 * pair, 0) // 4
 
             def block_step(b, carry):
                 @pl.when(c <= last_chunk(b))
@@ -419,7 +423,7 @@
 
             return lax.fori_loop(0, 2, block_step, carry)
 
-        return lax.fori_loop(0, 4, chunk_step, carry)
+        return lax.fori_loop(0, 2, pair_step, carry)
 
     lax.fori_loop(0, 4, column_step, 0)
 
@@ -442,11 +446,14 @@
                 part = full[(k + 2) * GROUP : (k + 3) * GROUP]
                 tangent = (part[:, :WIDTH] - part[:, WIDTH:] * attended) * share_scaled
                 tangent = jnp.where(valid, tangent, 0.0)
-                cot[b, g, k * GROUP : (k + 1) * GROUP] = tangent.astype(BF16)
-                corr[b, g, k * GROUP : (k + 1) * GROUP] = jnp.broadcast_to(
+                at = k * ROWS + g * GROUP
+                cot[b, at : at + GROUP] = tangent.astype(BF16)
+                corr[b, at : at + GROUP] = jnp.broadcast_to(
                     jnp.sum(tangent * attended, axis=1, keepdims=True), (GROUP, WIDTH)
                 )
-            inv[b, g] = share * (query_scale * adapter_scale / (SEQ * ROWS))
+            inv[b, g * GROUP : (g + 1) * GROUP] = share * (
+                query_scale * adapter_scale / (SEQ * ROWS)
+            )
         return carry
 
     lax.fori_loop(0, 2, turn, 0)
@@ -454,21 +461,16 @@
     grad[...] = jnp.zeros(grad.shape, F32)
 
     def second_pass(b, c):
-        keys = keys_of(c)
-        values = values_of(c)
-        for g in range(GROUPS):
-            aligned = nt(cot[b, g], values)
-            sloped = slopes[b, c, g]
-            parts = []
-            for k in range(PROBES):
-                level = corr[b, g, k * GROUP : (k + 1) * GROUP]
-                level = jnp.concatenate([level, level], axis=1)
-                parts.append(
-                    (sloped * (aligned[k * GROUP : (k + 1) * GROUP] - level)).astype(
-                        BF16
-                    )
-                )
-            grad[b, g] += nn(jnp.concatenate(parts, axis=0), keys)
+        aligned = nt(cot[b], values_of(c))
+        sloped = slopes[b, c]
+        parts = []
+        for k in range(PROBES):
+            level = corr[b, k * ROWS : (k + 1) * ROWS]
+            level = jnp.concatenate([level] * (CHUNK // WIDTH), axis=1)
+            parts.append(
+                (sloped * (aligned[k * ROWS : (k + 1) * ROWS] - level)).astype(BF16)
+            )
+        grad[b] += nn(jnp.concatenate(parts, axis=0), keys_of(c))
 
     def second_block(b, carry):
         def step(c, carry):
@@ -484,9 +486,7 @@
     for k in range(PROBES):
         stack = jnp.concatenate(
             [
-                grad[b, g, k * GROUP : (k + 1) * GROUP] * inv[b, g]
-                for b in range(2)
-                for g in range(GROUPS)
+                grad[b, k * ROWS : (k + 1) * ROWS] * inv[b] for b in range(2)
             ],
             axis=0,
         )
@@ -537,7 +537,9 @@
     pick = (lane == iota((PROBES, LANES), 0) + NB).astype(F32)
     small = nt(jnp.concatenate([quad, pick], axis=0), known, HIGHEST)
     gram = dots[:, KNOWN : KNOWN + PROBES] - small[0:PROBES]
-    diag_ref[0] = small[PROBES:]
+    out_ref[4:8] = jnp.concatenate(
+        [small[PROBES:], jnp.zeros((PROBES, LANES - PROBES), F32)], axis=1
+    )
 
     low = [[None] * PROBES for _ in range(PROBES)]
     for j in range(PROBES):
@@ -550,12 +552,12 @@
             for m in range(j):
                 entry = entry - low[i][m] * low[j][m]
             low[i][j] = entry / low[j][j]
-    row4, col4 = iota((PROBES, PROBES), 0), iota((PROBES, PROBES), 1)
-    upper = jnp.zeros((PROBES, PROBES), F32)
+    row4, col4 = iota((PROBES, LANES), 0), iota((PROBES, LANES), 1)
+    upper = jnp.zeros((PROBES, LANES), F32)
     for i in range(PROBES):
         for j in range(i + 1):
             upper = jnp.where((row4 == j) & (col4 == i), low[i][j], upper)
-    sub_ref[0] = upper
+    out_ref[8:12] = upper
 
     mix = jnp.where(
         lane < KNOWN,
@@ -576,11 +578,7 @@
         for k in range(1, PROBES):
             row = jnp.where(lane1 == k, rows[k][:, d * LANES : (d + 1) * LANES], row)
         made.append(row)
-    made = jnp.concatenate(made, axis=0)
-    for k in range(PROBES):
-        for h in range(2):
-            at = k * 32 + h * 16
-            next_ref[k, h] = made[:, at : at + 16]
+    out_ref[0:4] = jnp.concatenate(made, axis=0)
 
     shards = kv.at[pl.ds(0, SEQ - 1)]
     pltpu.make_async_copy(shards, shards, kv_send).wait()
@@ -588,6 +586,15 @@
     lr_copy.wait_send()
     for n, into in enumerate((lr_in, vt_in, g_in, h_in, w_in, e_in, c_in, d_in)):
         sent(into, n)
+
+
+def unpack(packed, next_ref, diag_ref, sub_ref):
+    for k in range(PROBES):
+        for h in range(2):
+            at = k * 32 + h * 16
+            next_ref[k, h] = packed[0:4, at : at + 16]
+    diag_ref[0] = packed[4:8, 0:PROBES]
+    sub_ref[0] = packed[8:12, 0:PROBES]
 
 
 def on_device(
@@ -608,17 +615,13 @@
     by_seq = pltpu.VMEM((SEQ,) + piece, F32)
     by_tensor = pltpu.VMEM((tensor,) + piece, F32)
     one = pltpu.VMEM(piece, F32)
-    turned, diag, sub = pl.pallas_call(
+    packed = pl.pallas_call(
         functools.partial(kernel, tensor),
-        out_shape=(
-            jax.ShapeDtypeStruct((PROBES, 2, 4, RANK), F32),
-            jax.ShapeDtypeStruct((1, PROBES, PROBES), F32),
-            jax.ShapeDtypeStruct((1, PROBES, PROBES), F32),
-        ),
+        out_shape=jax.ShapeDtypeStruct((16, LANES), F32),
         in_specs=[anywhere] * 5
         + [pl.BlockSpec(memory_space=pltpu.SMEM)]
         + [anywhere] * 2,
-        out_specs=(in_vmem,) * 3,
+        out_specs=in_vmem,
         scratch_shapes=[
             pltpu.VMEM((width, ROWS), BF16),
             pltpu.VMEM((RANK, width), BF16),
@@ -630,11 +633,11 @@
             pltpu.VMEM((SEQ, 2, ROWS, WIDTH), BF16),
             pltpu.VMEM((2, GROUPS, (PROBES + 1) * GROUP, WIDTH), BF16),
             pltpu.VMEM((2, GROUPS, (PROBES + 2) * GROUP, 2 * WIDTH), F32),
-            pltpu.VMEM((2, CHIPS, GROUPS, GROUP, CHUNK), F32),
-            pltpu.VMEM((2, GROUPS, PROBES * GROUP, WIDTH), BF16),
-            pltpu.VMEM((2, GROUPS, PROBES * GROUP, WIDTH), F32),
-            pltpu.VMEM((2, GROUPS, GROUP, WIDTH), F32),
-            pltpu.VMEM((2, GROUPS, PROBES * GROUP, WIDTH), F32),
+            pltpu.VMEM((2, CHUNKS, ROWS, CHUNK), F32),
+            pltpu.VMEM((2, PROBES * ROWS, WIDTH), BF16),
+            pltpu.VMEM((2, PROBES * ROWS, WIDTH), F32),
+            pltpu.VMEM((2, ROWS, WIDTH), F32),
+            pltpu.VMEM((2, PROBES * ROWS, WIDTH), F32),
             pltpu.VMEM((LANES, WIDTH), F32),
             pltpu.VMEM((LANES, WIDTH), F32),
             pltpu.VMEM((LANES, 4 * LANES), F32),
@@ -667,9 +670,19 @@
             pltpu.SemaphoreType.DMA((8,)),
         ],
         compiler_params=pltpu.CompilerParams(
-            collective_id=0, has_side_effects=True, vmem_limit_bytes=40 * 1024 * 1024
+            collective_id=0, has_side_effects=True, vmem_limit_bytes=60 * 1024 * 1024
         ),
     )(act, down, q, k, v, sequence_lengths, probe_in, basis_in)
+    turned, diag, sub = pl.pallas_call(
+        unpack,
+        out_shape=(
+            jax.ShapeDtypeStruct((PROBES, 2, 4, RANK), F32),
+            jax.ShapeDtypeStruct((1, PROBES, PROBES), F32),
+            jax.ShapeDtypeStruct((1, PROBES, PROBES), F32),
+        ),
+        in_specs=[in_vmem],
+        out_specs=(in_vmem,) * 3,
+    )(packed)
     return turned.transpose(0, 3, 1, 2)[None], diag, sub
 
 

time: 89.1 us -> 66.2 us (0.74)
  Pallas kernels: 80.7 us -> 64.7 us
  local copies, waits for them, and re-layouts: 6.6 us -> 0 us
    pallas_call x1 -> x2, Pallas kernels: 80.7 us -> 64.7 us  [the longest x1 63.4 us: on_device(): pl.pallas_call(functools.partial(kernel, tensor), out_shape=jax.ShapeDtyp...]
    unnamed x17 -> x0, local copies, waits for them, and re-layouts: 6.6 us -> none
where the time goes in v2:
time: 66.2 us; the launch traced here: 66 us
  Pallas kernels  64.7 us (98%)
  between operations  1.29 us (2%)
    pallas_call x1, Pallas kernels, on_device(): pl.pallas_call(functools.partial(kernel, tensor), out_shape=jax.ShapeDtyp...  63.4 us
    pallas_call x1, Pallas kernels, on_device(): pl.pallas_call(unpack, out_shape=(jax.ShapeDtypeStruct((PROBES, 2, 4, RAN...  1.38 us

profile of v2, /device:TPU:1, one launch (start us, length us, event | category | flops | bytes accessed | tf_op | source)
XLA Modules:
  0.0 66.0 jit_solution(8508634944647091558)
XLA Ops:
  1.3 63.4 %shard_map.103.packed = f32[16,128]{1,0:T(8,128)} custom-call(bf16[288,128]{1,0:T(8,128)(2,1)} %bitcast.14, bf16[16,288]{1,0:T(8,128)(2,1)} %bitcast.20, bf16[256,128]{1,0:T(8,128)(2,1)} %bitcast.15, bf16[128,128]{1,0:T(8,128)(2,1)} %bitcast.17, bf16[128,128]{1,0:T(8,128)(2,1)} %bitcast.18, s32[1]{0:T(128)S(6)} %copy.11.len_ref, f32[4,2,4,16]{3,2,1,0:T(4,128)} %bitcast.19, ...), custom_call_target="tpu_custom_call" | custom-call | tf_op jit(solution)/shard_map/pallas_call | solution.py:618
  64.7 1.4 %shard_map.104 = (f32[4,2,4,16]{3,2,1,0:T(4,128)}, f32[1,4,4]{2,1,0:T(4,128)}, f32[1,4,4]{2,1,0:T(4,128)}) custom-call(f32[16,128]{1,0:T(8,128)} %shard_map.103.packed), custom_call_target="tpu_custom_call" | custom-call | tf_op jit(solution)/shard_map/pallas_call | solution.py:676

commit v3 on v2

--- a/solution.py
+++ b/solution.py
@@ -207,10 +207,10 @@
         pltpu.make_async_copy(span, span, ex_send.at[n]).wait()
 
     def total(into):
-        out = into[0]
-        for i in range(1, into.shape[0]):
-            out = out + into[i]
-        return out
+        terms = [into[i] for i in range(into.shape[0])]
+        while len(terms) > 1:
+            terms = [u + v for u, v in zip(terms[::2], terms[1::2])]
+        return terms[0]
 
     def push(src, to, sem):
         pltpu.make_async_remote_copy(
@@ -229,27 +229,41 @@
     x_up, x_down = seq_at(x + 1, z, core), seq_at(x + 3, z, core)
     sibling = seq_at(x, z, 1 - core)
 
-    def push_column(d):
-        src = kv.at[seq_at(x, z + d, core)]
-        push(src, x_up, x_recv.at[d, 0])
-        push(src, x_down, x_recv.at[d, 1])
-        push(src, sibling, sib_recv.at[0, d])
+    def push_column(d, j):
+        src = kv.at[seq_at(x, z + d, core), j]
+        if j == 0:
+            push(src, x_up, x_recv.at[d, 0])
+            push(src, x_down, x_recv.at[d, 2])
+        else:
+            push(src, x_down, x_recv.at[d, 3])
+            push(src, x_up, x_recv.at[d, 1])
+        push(src, sibling, sib_recv.at[0, d, j])
+
+    def take_below(d, j):
+        half = kv.at[seq_at(x + 3, z + d, core), j]
+        came(half, x_recv.at[d, j])
+        if j == 0:
+            push(half, x_up, x_recv.at[d, 4])
+        push(half, sibling, sib_recv.at[3, d, j])
+
+    def take_above(d, j):
+        half = kv.at[seq_at(x + 1, z + d, core), j]
+        came(half, x_recv.at[d, 2 + j])
+        if j == 1:
+            push(half, x_down, x_recv.at[d, 5])
+        push(half, sibling, sib_recv.at[1, d, j])
 
     def pass_x(d):
-        below = seq_at(x + 3, z + d, core)
-        came(kv.at[below], x_recv.at[d, 0])
-        push(kv.at[below, 0], x_up, x_recv.at[d, 2])
-        push(kv.at[below], sibling, sib_recv.at[3, d])
-        above = seq_at(x + 1, z + d, core)
-        came(kv.at[above], x_recv.at[d, 1])
-        push(kv.at[above, 1], x_down, x_recv.at[d, 3])
-        push(kv.at[above], sibling, sib_recv.at[1, d])
+        take_below(d, 0)
+        take_above(d, 1)
+        take_below(d, 1)
+        take_above(d, 0)
 
     def pass_far(d):
-        far = seq_at(x + 2, z + d, core)
-        came(kv.at[far, 0], x_recv.at[d, 2])
-        came(kv.at[far, 1], x_recv.at[d, 3])
-        push(kv.at[far], sibling, sib_recv.at[2, d])
+        for j in range(2):
+            half = kv.at[seq_at(x + 2, z + d, core), j]
+            came(half, x_recv.at[d, 4 + j])
+            push(half, sibling, sib_recv.at[2, d, j])
 
     loads[0].wait()
     loads[1].wait()
@@ -289,10 +303,12 @@
     loads[6].wait()
 
     pl.semaphore_wait(barrier, SEQ - 1 + tensor - 1)
-    mine = kv.at[s]
-    push(mine, z_up, z_recv.at[0])
-    push(mine, z_down, z_recv.at[1])
-    push_column(0)
+    push(kv.at[s, 0], z_up, z_recv.at[0])
+    push(kv.at[s, 1], z_down, z_recv.at[3])
+    push(kv.at[s, 1], z_up, z_recv.at[1])
+    push(kv.at[s, 0], z_down, z_recv.at[2])
+    push_column(0, 0)
+    push_column(0, 1)
     send_tensor(lr_out, lr_in, 0)
     send_seq(lambda to: vt_out, vt_in, 1)
     q_copy = pltpu.make_async_remote_copy(
@@ -306,14 +322,21 @@
     q_copy.start()
 
     below = seq_at(x, z + 3, core)
-    came(kv.at[below], z_recv.at[0])
-    push(kv.at[below, 0], z_up, z_recv.at[2])
-    push_column(3)
     above = seq_at(x, z + 1, core)
-    came(kv.at[above], z_recv.at[1])
-    push(kv.at[above, 1], z_down, z_recv.at[3])
-    push_column(1)
-    pass_x(0)
+    take_below(0, 0)
+    take_above(0, 1)
+    came(kv.at[below, 0], z_recv.at[0])
+    push(kv.at[below, 0], z_up, z_recv.at[4])
+    push_column(3, 0)
+    came(kv.at[above, 1], z_recv.at[3])
+    push(kv.at[above, 1], z_down, z_recv.at[5])
+    push_column(1, 1)
+    came(kv.at[below, 1], z_recv.at[1])
+    push_column(3, 1)
+    came(kv.at[above, 0], z_recv.at[2])
+    push_column(1, 0)
+    take_below(0, 1)
+    take_above(0, 0)
 
     arrived(lr_in, 0)
     lr[0] = total(lr_in)
@@ -328,9 +351,10 @@
     lr_copy.start()
 
     far = seq_at(x, z + 2, core)
-    came(kv.at[far, 0], z_recv.at[2])
-    came(kv.at[far, 1], z_recv.at[3])
-    push_column(2)
+    came(kv.at[far, 0], z_recv.at[4])
+    push_column(2, 0)
+    came(kv.at[far, 1], z_recv.at[5])
+    push_column(2, 1)
     pass_far(0)
     pass_x(3)
     pass_x(1)
@@ -411,7 +435,9 @@
             pair = lax.rem(z // 2 + p, 2)
             for i in range(2):
                 other = seq_at(x + e, 2 * pair + i, 1 - core)
-                came(kv.at[other], sib_recv.at[e, lax.rem(2 * pair + i - z + 4, 4)])
+                d = lax.rem(2 * pair + i - z + 4, 4)
+                came(kv.at[other, 0], sib_recv.at[e, d, 0])
+                came(kv.at[other, 1], sib_recv.at[e, d, 1])
             c = seq_at(x + e, 2 * pair, 0) // 4
 
             def block_step(b, carry):
@@ -460,24 +486,33 @@
 
     grad[...] = jnp.zeros(grad.shape, F32)
 
+    def two(part, c):
+        return jnp.concatenate([part(2 * c), part(2 * c + 1)], axis=0)
+
     def second_pass(b, c):
-        aligned = nt(cot[b], values_of(c))
-        sloped = slopes[b, c]
+        aligned = nt(cot[b], two(values_of, c))
+        sloped = jnp.concatenate([slopes[b, 2 * c], slopes[b, 2 * c + 1]], axis=1)
         parts = []
         for k in range(PROBES):
             level = corr[b, k * ROWS : (k + 1) * ROWS]
-            level = jnp.concatenate([level] * (CHUNK // WIDTH), axis=1)
+            level = jnp.concatenate([level] * (2 * CHUNK // WIDTH), axis=1)
             parts.append(
                 (sloped * (aligned[k * ROWS : (k + 1) * ROWS] - level)).astype(BF16)
             )
-        grad[b] += nn(jnp.concatenate(parts, axis=0), keys_of(c))
+        grad[b] += nn(jnp.concatenate(parts, axis=0), two(keys_of, c))
 
     def second_block(b, carry):
         def step(c, carry):
             second_pass(b, c)
             return carry
 
-        return lax.fori_loop(0, last_chunk(b) + 1, step, carry)
+        last = last_chunk(b)
+
+        @pl.when(last % 2 == 0)
+        def _():
+            slopes[b, last + 1] = jnp.zeros((ROWS, CHUNK), F32)
+
+        return lax.fori_loop(0, last // 2 + 1, step, carry)
 
     lax.fori_loop(0, 2, second_block, 0)
 
@@ -661,9 +696,9 @@
             by_seq,
             pltpu.SemaphoreType.DMA((7,)),
             pltpu.SemaphoreType.DMA,
-            pltpu.SemaphoreType.DMA((4,)),
-            pltpu.SemaphoreType.DMA((4, 4)),
-            pltpu.SemaphoreType.DMA((4, 4)),
+            pltpu.SemaphoreType.DMA((6,)),
+            pltpu.SemaphoreType.DMA((4, 6)),
+            pltpu.SemaphoreType.DMA((4, 4, 2)),
             pltpu.SemaphoreType.DMA((2,)),
             pltpu.SemaphoreType.DMA((2,)),
             pltpu.SemaphoreType.DMA((8,)),

time: 66.2 us -> 64.8 us (0.979)
  Pallas kernels: 64.7 us -> 63.3 us
    pallas_call x1, Pallas kernels: 63.4 us -> 61.9 us  [on_device(): pl.pallas_call(functools.partial(kernel, tensor), out_shape=jax.ShapeDtyp...]
where the time goes in v3:
time: 64.8 us; the launch traced here: 64.6 us
  Pallas kernels  63.3 us (98%)
  between operations  1.29 us (2%)
    pallas_call x1, Pallas kernels, on_device(): pl.pallas_call(functools.partial(kernel, tensor), out_shape=jax.ShapeDtyp...  61.9 us
    pallas_call x1, Pallas kernels, on_device(): pl.pallas_call(unpack, out_shape=(jax.ShapeDtypeStruct((PROBES, 2, 4, RAN...  1.38 us

profile of v3, /device:TPU:1, one launch (start us, length us, event | category | flops | bytes accessed | tf_op | source)
XLA Modules:
  0.0 64.6 jit_solution(18044884844948141709)
XLA Ops:
  1.3 61.9 %shard_map.103.packed = f32[16,128]{1,0:T(8,128)} custom-call(bf16[288,128]{1,0:T(8,128)(2,1)} %bitcast.14, bf16[16,288]{1,0:T(8,128)(2,1)} %bitcast.20, bf16[256,128]{1,0:T(8,128)(2,1)} %bitcast.15, bf16[128,128]{1,0:T(8,128)(2,1)} %bitcast.17, bf16[128,128]{1,0:T(8,128)(2,1)} %bitcast.18, s32[1]{0:T(128)S(6)} %copy.11.len_ref, f32[4,2,4,16]{3,2,1,0:T(4,128)} %bitcast.19, ...), custom_call_target="tpu_custom_call" | custom-call | tf_op jit(solution)/shard_map/pallas_call | solution.py:653
  63.2 1.4 %shard_map.104 = (f32[4,2,4,16]{3,2,1,0:T(4,128)}, f32[1,4,4]{2,1,0:T(4,128)}, f32[1,4,4]{2,1,0:T(4,128)}) custom-call(f32[16,128]{1,0:T(8,128)} %shard_map.103.packed), custom_call_target="tpu_custom_call" | custom-call | tf_op jit(solution)/shard_map/pallas_call | solution.py:711

commit v4 on v3

--- a/solution.py
+++ b/solution.py
@@ -171,7 +171,7 @@
 
     def send_seq(src_of, into, n):
         def body(o, carry):
-            to = lax.rem(s + o, SEQ)
+            to = lax.rem(s + 1 + lax.rem(o + 14, SEQ - 1), SEQ)
             pltpu.make_async_remote_copy(
                 src_ref=src_of(to),
                 dst_ref=into.at[s],

time: 64.8 us -> 64.3 us (level)
  no operation moved by 1% of the time
where the time goes in v4:
time: 64.3 us; the launch traced here: 64.1 us
  Pallas kernels  62.8 us (98%)
  between operations  1.29 us (2%)
    pallas_call x1, Pallas kernels, on_device(): pl.pallas_call(functools.partial(kernel, tensor), out_shape=jax.ShapeDtyp...  61.4 us
    pallas_call x1, Pallas kernels, on_device(): pl.pallas_call(unpack, out_shape=(jax.ShapeDtypeStruct((PROBES, 2, 4, RAN...  1.38 us

profile of v4, /device:TPU:1, one launch (start us, length us, event | category | flops | bytes accessed | tf_op | source)
XLA Modules:
  0.0 64.1 jit_solution(9660279993475913418)
XLA Ops:
  1.3 61.4 %shard_map.103.packed = f32[16,128]{1,0:T(8,128)} custom-call(bf16[288,128]{1,0:T(8,128)(2,1)} %bitcast.14, bf16[16,288]{1,0:T(8,128)(2,1)} %bitcast.20, bf16[256,128]{1,0:T(8,128)(2,1)} %bitcast.15, bf16[128,128]{1,0:T(8,128)(2,1)} %bitcast.17, bf16[128,128]{1,0:T(8,128)(2,1)} %bitcast.18, s32[1]{0:T(128)S(6)} %copy.11.len_ref, f32[4,2,4,16]{3,2,1,0:T(4,128)} %bitcast.19, ...), custom_call_target="tpu_custom_call" | custom-call | tf_op jit(solution)/shard_map/pallas_call | solution.py:653
  62.7 1.4 %shard_map.104 = (f32[4,2,4,16]{3,2,1,0:T(4,128)}, f32[1,4,4]{2,1,0:T(4,128)}, f32[1,4,4]{2,1,0:T(4,128)}) custom-call(f32[16,128]{1,0:T(8,128)} %shard_map.103.packed), custom_call_target="tpu_custom_call" | custom-call | tf_op jit(solution)/shard_map/pallas_call | solution.py:711
